TPU v7x, 256 devices: a whole 4x4x8 slice. The times are simulated.
256 devices in a mesh: gx: 16 (over z, core), gy: 16 (over y, x).
Axes of the slice: x: 4, y: 4, z: 8, core: 2. Of those that a mesh axis runs over, the one named last changes fastest.
Arguments:
- tokens: bfloat16 [1024, 16384], P('gy', 'gx'), may hold values from -6 to 6
- gate_weight: bfloat16 [16384, 26624], P('gx', 'gy'), may hold values from -0.046875 to 0.046875
- up_weight: bfloat16 [16384, 26624], P('gx', 'gy'), may hold values from -0.046875 to 0.046875
- down_weight: bfloat16 [26624, 16384], P('gy', 'gx'), may hold values from -0.0390625 to 0.0390625
Outputs:
- mixed: float32 [1024, 16384], P('gy', 'gx')
All inputs are finite; a program needn't handle non-finite values.
Results may differ from a plain program's by a relative error of at most 0.0029.
Values may be sent and summed in bfloat16 or wider, within the bound.
A program may use at most 128 MiB of HBM per device.

v0:
```python
import jax
import jax.numpy as jnp
from jax import lax
from jax.sharding import PartitionSpec as P


def local(tokens, gate_weight, up_weight, down_weight):
    all_rows = lax.all_gather(tokens, "gy", axis=0, tiled=True)
    width = gate_weight.shape[1]
    rows = all_rows
    gate_part = jnp.dot(rows, gate_weight, preferred_element_type=jnp.float32)
    up_part = jnp.dot(rows, up_weight, preferred_element_type=jnp.float32)
    shares = lax.psum_scatter(
        jnp.concatenate([gate_part, up_part], axis=1), "gx", scatter_dimension=0, tiled=True
    )
    hidden_share = (jax.nn.silu(shares[:, :width]) * shares[:, width:]).astype(jnp.bfloat16)
    hidden = lax.all_gather(hidden_share, "gx", axis=0, tiled=True)
    rows = hidden
    return lax.psum_scatter(
        jnp.dot(rows, down_weight, preferred_element_type=jnp.float32),
        "gy",
        scatter_dimension=0,
        tiled=True,
    )


def solution(mesh):
    placed = (P("gy", "gx"), P("gx", "gy"), P("gx", "gy"), P("gy", "gx"))
    return jax.shard_map(
        local, mesh=mesh, in_specs=placed, out_specs=P("gy", "gx"), check_vma=False
    )
```

profile of v0, /device:TPU:1, one launch (start us, length us, event | category | flops | bytes accessed | tf_op | source)
XLA Modules:
  0.0 300.7 jit_solution(10688174737838095466)
XLA Ops:
  6.5 0.0 copy-start
  6.5 0.0 all-gather.3.cloned.1.call-start
  6.5 0.7 all-gather.3.cloned.1.call-update
  7.3 0.0 reduce-scatter.3.cloned.1.call-start
  7.3 55.4 %all-gather.3.cloned.1.call-done = bf16[1024,1024]{1,0:T(8,128)(2,1)} async-done(((bf16[64,1024]{1,0:T(8,128)(2,1)}), bf16[1024,1024]{1,0:T(8,128)(2,1)}) %all-gather.3.cloned.1.call-update) | async-done | bytes 2097168 | tf_op jit(solution)/shard_map/all_gather | solution.py:8
  62.7 0.0 copy-done
  62.7 0.0 copy-start.1
  62.7 0.0 copy-start.2
  62.7 5.7 %fusion.2 = f32[1024,1664]{1,0:T(8,128)S(1)} fusion(bf16[1024,1024]{1,0:T(8,128)(2,1)} %all-gather.3.cloned.1.call-done, bf16[1024,1664]{1,0:T(8,128)(2,1)S(1)} %copy-done), kind=kOutput, calls=%fused_computation.4 | convolution fusion | flops 3489660928 | bytes 12320768 | tf_op jit(solution)/shard_map/dot_general | solution.py:12
  68.4 0.0 copy-done.1
  68.4 0.0 copy-done.2
  68.5 4.0 %fusion.1 = f32[1024,1664]{1,0:T(8,128)S(1)} fusion(bf16[1024,1024]{1,0:T(8,128)(2,1)S(1)} %copy-done.2, bf16[1024,1664]{1,0:T(8,128)(2,1)S(1)} %copy-done.1), kind=kOutput, calls=%fused_computation.3 | convolution fusion | flops 3489660928 | bytes 12320768 | tf_op jit(solution)/shard_map/dot_general | solution.py:11
  72.4 5.2 %pad_maximum_fusion = f32[1024,3328]{1,0:T(8,128)} fusion(f32[1024,1664]{1,0:T(8,128)S(1)} %fusion.2, f32[1024,1664]{1,0:T(8,128)S(1)} %fusion.1), kind=kLoop, calls=%fused_computation | loop fusion | flops 3407872 | bytes 27262976 | tf_op jit(solution)/shard_map/concatenate | solution.py:14
  77.7 0.0 reduce-scatter.3.cloned.1.call-update
  77.7 0.0 all-gather.5.cloned.1.call-start
  77.8 83.9 %reduce-scatter.3.cloned.1.call-done = f32[64,3328]{1,0:T(8,128)} async-done(((f32[1024,3328]{1,0:T(8,128)}), f32[64,3328]{1,0:T(8,128)}) %reduce-scatter.3.cloned.1.call-update) | async-done | bytes 851984 | tf_op jit(solution)/shard_map/reduce_scatter | solution.py:13
  161.7 1.9 fusion
  163.6 0.0 all-gather.5.cloned.1.call-update
  163.6 0.0 reduce-scatter.5.cloned.1.call-start
  163.7 42.2 %all-gather.5.cloned.1.call-done = bf16[1024,1664]{1,0:T(8,128)(2,1)} async-done(((bf16[64,1664]{1,0:T(8,128)(2,1)}), bf16[1024,1664]{1,0:T(8,128)(2,1)}) %all-gather.5.cloned.1.call-update) | async-done | bytes 3407888 | tf_op jit(solution)/shard_map/all_gather | solution.py:17
  205.8 8.9 %fusion.3 = f32[1024,1024]{1,0:T(8,128)} fusion(bf16[1024,1664]{1,0:T(8,128)(2,1)} %all-gather.5.cloned.1.call-done, bf16[1664,1024]{1,0:T(8,128)(2,1)} %param.7), kind=kOutput, calls=%fused_computation.5 | convolution fusion | flops 3489660928 | bytes 11010048 | tf_op jit(solution)/shard_map/dot_general | solution.py:20
  214.7 0.0 reduce-scatter.5.cloned.1.call-update
  214.8 79.4 %reduce-scatter.5.cloned.1.call-done = f32[64,1024]{1,0:T(8,128)} async-done(((f32[1024,1024]{1,0:T(8,128)}), f32[64,1024]{1,0:T(8,128)}) %reduce-scatter.5.cloned.1.call-update) | async-done | bytes 262160 | tf_op jit(solution)/shard_map/reduce_scatter | solution.py:19
Async XLA Ops:
  6.5 56.2 %copy-start = (bf16[1024,1664]{1,0:T(8,128)(2,1)S(1)}, bf16[1024,1664]{1,0:T(8,128)(2,1)}, u32[]{:S(2)}) copy-start(bf16[1024,1664]{1,0:T(8,128)(2,1)} %param.6) | copy-start | bytes 10223620
  6.5 56.2 %all-gather.3.cloned.1.call-start = ((), (), s32[]{:S(2)}) async-start(), calls=%async_computation.2 | async-start | bytes 2228224 | tf_op jit(solution)/shard_map/all_gather | solution.py:8
  7.3 154.4 %reduce-scatter.3.cloned.1.call-start = ((), (), s32[]{:S(2)}) async-start(), calls=%async_computation.3 | async-start | bytes 14483456 | tf_op jit(solution)/shard_map/reduce_scatter | solution.py:13
  62.7 5.7 %copy-start.1 = (bf16[1024,1664]{1,0:T(8,128)(2,1)S(1)}, bf16[1024,1664]{1,0:T(8,128)(2,1)}, u32[]{:S(2)}) copy-start(bf16[1024,1664]{1,0:T(8,128)(2,1)} %param.5) | copy-start | bytes 10223620
  62.7 5.7 %copy-start.2 = (bf16[1024,1024]{1,0:T(8,128)(2,1)S(1)}, bf16[1024,1024]{1,0:T(8,128)(2,1)}, u32[]{:S(2)}) copy-start(bf16[1024,1024]{1,0:T(8,128)(2,1)} %all-gather.3.cloned.1.call-done) | copy-start | bytes 6291460
  77.7 128.1 %all-gather.5.cloned.1.call-start = ((), (), s32[]{:S(2)}) async-start(), calls=%async_computation.4 | async-start | bytes 3620864 | tf_op jit(solution)/shard_map/all_gather | solution.py:17
  163.6 130.6 %reduce-scatter.5.cloned.1.call-start = ((), (), s32[]{:S(2)}) async-start(), calls=%async_computation.5 | async-start | bytes 4456448 | tf_op jit(solution)/shard_map/reduce_scatter | solution.py:19
Sparse Core Ops, SparseCore 0:
  9.8 52.8 all-gather.2
  77.8 83.7 reduce-scatter.2
  163.7 42.0 all-gather.4
  214.9 79.2 reduce-scatter.4
where the time goes:
time: 301 us
  waiting for transfers between devices  262 us (87%)
  matrix products  18.6 us (6%)
  between operations  13.2 us (4%)
  other arithmetic  7.18 us (2%)
    reduce_scatter x1, waiting for transfers between devices, local(): lax.psum_scatter(jnp.concatenate([gate_part, up_part], axis=1), 'gx', sca...  83.9 us
    reduce_scatter x1, waiting for transfers between devices, local(): lax.psum_scatter(jnp.dot(rows, down_weight, preferred_element_type=jnp.fl...  79.4 us
    all_gather x1, waiting for transfers between devices, local(): all_rows = lax.all_gather(tokens, 'gy', axis=0, tiled=True)  55.4 us
    all_gather x1, waiting for transfers between devices, local(): hidden = lax.all_gather(hidden_share, 'gx', axis=0, tiled=True)  42.2 us
    dot_general x1, matrix products, local(): jnp.dot(rows, down_weight, preferred_element_type=jnp.float32)  8.9 us
  transfers between devices with their start and end apart: 4, of which 4 were waited for; matrix products, arithmetic and copies ran while one was open for 0% of the time, Pallas kernels for 0%

commit v1 on v0

v1 whole, which is shorter than its diff:
```python
import jax
import jax.numpy as jnp
from jax import lax
from jax.experimental import pallas as pl
from jax.experimental.pallas import tpu as pltpu
from jax.sharding import PartitionSpec as P

MESH = pl.DeviceIdType.MESH
Z = 8
ROWS = 64
HALF = 32
GATE, UP = 0, 1
LANES = 128
POWER = 7
SHIFT = 5.0


def encode(x):
    y = x * 32.0
    y2 = y * y
    y3 = y2 * y
    return (y2 * y2 * y3).astype(jnp.bfloat16)


def decode(v):
    y = v.astype(jnp.float32)
    root = jnp.exp2(jnp.log(jnp.abs(y)) * (1.4426950408889634 / POWER) - SHIFT)
    return jnp.where(y < 0.0, -root, root)


def kernel(
    tok_hbm, gate_hbm, up_hbm, down_hbm, out_ref,
    w, wd, tok, part, sib, zsend, zrecv, hid, msend, mrecv,
    lsem, tok_s, tok_r, ex_s, ex_r, rs_s, rs_r, ag_s, ag_r, sb_s, sb_r, mx_s, mx_r,
):
    gx, gy = lax.axis_index("gx"), lax.axis_index("gy")
    m, c = gx // 2, gx % 2
    gyy, gyx = gy // 4, gy % 4
    width = w.shape[2]
    tiles = width // LANES

    def at_xy(dy, dx):
        return {"gx": gx, "gy": ((gyy + dy + 8) % 4) * 4 + (gyx + dx + 8) % 4}

    def at_z(step):
        return {"gx": ((m + step + Z) % Z) * 2 + c, "gy": gy}

    other = {"gx": m * 2 + 1 - c, "gy": gy}

    def block(k):
        return (m + k + Z) % Z

    def shift_of(d, h):
        return d // 4 + 2 * h, d % 4 + 2 * h

    loads = [
        pltpu.make_async_copy(gate_hbm, w.at[GATE], lsem.at[0]),
        pltpu.make_async_copy(up_hbm, w.at[UP], lsem.at[1]),
        pltpu.make_async_copy(down_hbm, wd, lsem.at[2]),
        pltpu.make_async_copy(tok_hbm, tok.at[0], lsem.at[3]),
    ]
    for load in loads[:2] + loads[3:]:
        load.start()

    barrier = pltpu.get_barrier_semaphore()
    for there in (at_z(1), at_z(-1), other):
        pl.semaphore_signal(barrier, inc=1, device_id=there, device_id_type=MESH)
    for dy in range(4):
        for dx in range(4):
            if dy or dx:
                pl.semaphore_signal(barrier, inc=1, device_id=at_xy(dy, dx), device_id_type=MESH)
    pl.semaphore_wait(barrier, 18)

    order = [4, 3, -3, 2, -2, 1, -1, 0]

    def tok_copy(k, h):
        d = block(k)
        j = d * 2 + h
        dy, dx = shift_of(d, h)
        return j, pltpu.make_async_remote_copy(
            src_ref=tok_hbm, dst_ref=tok.at[j], send_sem=tok_s.at[j], recv_sem=tok_r.at[j],
            device_id=at_xy(-dy, -dx), device_id_type=MESH,
        )

    def tok_send(k):
        for h in range(2):
            j, copy = tok_copy(k, h)

            @pl.when(j != 0)
            def _():
                copy.start()

    def tok_wait(k):
        for h in range(2):
            j, copy = tok_copy(k, h)

            @pl.when(j != 0)
            def _():
                copy.wait_recv()

    def exchange(b, gu):
        return pltpu.make_async_remote_copy(
            src_ref=part.at[b, gu, :, pl.ds((1 - c) * HALF, HALF), :], dst_ref=sib.at[b, gu],
            send_sem=ex_s.at[b * 2 + gu], recv_sem=ex_r.at[b * 2 + gu], device_id=other, device_id_type=MESH,
        )

    def product(b, gu):
        d = block(order[b])
        wide = 2 * LANES

        def tile(start, size):
            rows = jnp.concatenate([tok[d * 2], tok[d * 2 + 1]], axis=0)
            res = jnp.dot(rows, w[gu, :, pl.ds(start, size)], preferred_element_type=jnp.float32)
            part[b, gu, 0, :, pl.ds(start, size)] = res[:ROWS]
            part[b, gu, 1, :, pl.ds(start, size)] = res[ROWS:]

        def body(i, _):
            tile(pl.multiple_of(i * wide, wide), wide)
            return 0

        lax.fori_loop(0, width // wide, body, 0)
        if width % wide:
            tile(width - width % wide, width % wide)
        exchange(b, gu).start()

    def unit_index(k, q, h):
        return h if k == 4 else 2 + (3 - k) * 4 + h * 2 + q

    def rs_copy(way, k, q, h):
        u = unit_index(k, q, h)
        return pltpu.make_async_remote_copy(
            src_ref=zsend.at[way, u], dst_ref=zrecv.at[way, u],
            send_sem=rs_s.at[way * 14 + u], recv_sem=rs_r.at[way * 14 + u],
            device_id=at_z(1 - 2 * way), device_id_type=MESH,
        )

    def matrix_of(way, q):
        return (UP, GATE)[q] if way == 0 else (GATE, UP)[q]

    def own_sum(b, gu, h, cols):
        return part[b, gu, h, pl.ds(c * HALF, HALF), cols] + sib[b, gu, h, :, cols]

    def combine(b, way, k, q, h):
        gu = matrix_of(way, q)
        arrived = (k + 1 < 4) or (k + 1 == 4 and q == 1)
        if arrived:
            rs_copy(way, k + 1, q, h).wait_recv()
            src = unit_index(k + 1, q, h)
        u = unit_index(k, q, h)
        for i in range(tiles):
            cols = pl.ds(i * LANES, LANES)
            total = own_sum(b, gu, h, cols)
            if arrived:
                total = total + decode(zrecv[way, src, :, cols])
            zsend[way, u, :, cols] = encode(total)
        rs_copy(way, k, q, h).start()

    def ag_copy(way, s, h):
        u = 6 if s == 4 else (s - 1) * 2 + h
        d = block(-(s - 1) if way == 0 else s - 1)
        place = hid.at[d, h, pl.ds(c * HALF, HALF), :]
        return pltpu.make_async_remote_copy(
            src_ref=place, dst_ref=place, send_sem=ag_s.at[way * 7 + u], recv_sem=ag_r.at[way * 7 + u],
            device_id=at_z(1 - 2 * way), device_id_type=MESH,
        )

    def ag_arrival(way, s, h):
        u = 6 if s == 4 else (s - 1) * 2 + h
        d = block(-s if way == 0 else s)
        place = hid.at[d, h, pl.ds(c * HALF, HALF), :]
        return pltpu.make_async_remote_copy(
            src_ref=place, dst_ref=place, send_sem=ag_s.at[way * 7 + u], recv_sem=ag_r.at[way * 7 + u],
            device_id=at_z(1 - 2 * way), device_id_type=MESH,
        )

    def sib_index(k, h):
        return order.index(k) * 2 + h

    def sib_copy(k, h, core):
        place = hid.at[block(k), h, pl.ds(core * HALF, HALF), :]
        i = sib_index(k, h)
        return pltpu.make_async_remote_copy(
            src_ref=place, dst_ref=place, send_sem=sb_s.at[i], recv_sem=sb_r.at[i],
            device_id=other, device_id_type=MESH,
        )

    def finish(h):
        for way in range(2):
            for q in range(2):
                rs_copy(way, 1, q, h).wait_recv()
        for i in range(tiles):
            cols = pl.ds(i * LANES, LANES)
            sums = []
            for gu in (GATE, UP):
                total = own_sum(7, gu, h, cols)
                for way in range(2):
                    q = 0 if matrix_of(way, 0) == gu else 1
                    total = total + decode(zrecv[way, unit_index(1, q, h), :, cols])
                sums.append(total)
            gate, up = sums
            hid[m, h, pl.ds(c * HALF, HALF), cols] = (gate / (1.0 + jnp.exp(-gate)) * up).astype(jnp.bfloat16)
        ag_copy(0, 1, h).start()
        ag_copy(1, 1, h).start()
        sib_copy(0, h, c).start()

    def mx_copy(k, h):
        d = block(k)
        j = d * 2 + h
        dy, dx = shift_of(d, h)
        return j, pltpu.make_async_remote_copy(
            src_ref=msend.at[j], dst_ref=mrecv.at[j], send_sem=mx_s.at[j], recv_sem=mx_r.at[j],
            device_id=at_xy(dy, dx), device_id_type=MESH,
        )

    def down(units):
        for k, h in units:
            sib_copy(k, h, 1 - c).wait_recv()
        wide = 2 * LANES

        def body(i, _):
            cols = pl.ds(pl.multiple_of(i * wide, wide), wide)
            rows = [hid[block(k), h] for k, h in units]
            rows = rows[0] if len(rows) == 1 else jnp.concatenate(rows, axis=0)
            res = jnp.dot(rows, wd[:, cols], preferred_element_type=jnp.float32).astype(jnp.bfloat16)
            for n, (k, h) in enumerate(units):
                msend[block(k) * 2 + h, :, cols] = res[n * ROWS : (n + 1) * ROWS]
            return 0

        lax.fori_loop(0, wd.shape[1] // wide, body, 0)
        for k, h in units:
            j, copy = mx_copy(k, h)

            @pl.when(j != 0)
            def _():
                copy.start()

            @pl.when(j == 0)
            def _():
                mrecv[0] = msend[0]

    tok_send(4)
    tok_send(3)
    tok_send(-3)
    loads[3].wait()
    tok_wait(4)
    for k in (2, -2, 1, -1, 0):
        tok_send(k)
    loads[0].wait()
    product(0, GATE)
    loads[1].wait()
    product(0, UP)
    loads[2].start()
    for gu, way in ((GATE, 0), (UP, 1)):
        exchange(0, gu).wait_recv()
        for h in range(2):
            combine(0, way, 4, 1, h)
    for k in (3, 2, 1):
        bs = (order.index(k), order.index(-k))
        tok_wait(k)
        tok_wait(-k)
        for q in range(2):
            for way in range(2):
                product(bs[way], matrix_of(way, q))
        for h in range(2):
            for q in range(2):
                for way in range(2):
                    if h == 0:
                        exchange(bs[way], matrix_of(way, q)).wait_recv()
                    combine(bs[way], way, k, q, h)
    tok_wait(0)
    for gu in range(2):
        product(7, gu)
    for gu in range(2):
        exchange(7, gu).wait_recv()
    finish(0)
    finish(1)
    loads[2].wait()
    waiting = [[(0, 0)], [(0, 1)]]
    for s in (1, 2, 3):
        for h in range(2):
            for way in range(2):
                ag_arrival(way, s, h).wait_recv()
                if s < 3 or way == h:
                    ag_copy(way, 4 if s == 3 else s + 1, h).start()
                sib_copy(-s if way == 0 else s, h, c).start()
            down(waiting.pop(0))
            waiting.append([(-s, h), (s, h)])
    for way in range(2):
        ag_arrival(way, 4, way).wait_recv()
        sib_copy(4, way, c).start()
    down(waiting.pop(0))
    down(waiting.pop(0))
    down([(4, 0), (4, 1)])

    for k in (0, -1, 1, -2, 2, -3, 3, 4):
        for h in range(2):
            j, copy = mx_copy(k, h)

            @pl.when(j != 0)
            def _():
                copy.wait_recv()

    def total_body(i, _):
        cols = pl.ds(pl.multiple_of(i * LANES, LANES), LANES)
        total = mrecv[0, :, cols].astype(jnp.float32)
        for j in range(1, 16):
            total = total + mrecv[j, :, cols].astype(jnp.float32)
        out_ref[:, cols] = total
        return 0

    lax.fori_loop(0, out_ref.shape[1] // LANES, total_body, 0)

    for k in order:
        for h in range(2):
            j, tcopy = tok_copy(k, h)
            _, mcopy = mx_copy(k, h)

            @pl.when(j != 0)
            def _():
                tcopy.wait_send()
                mcopy.wait_send()

            sib_copy(k, h, c).wait_send()
    for b in range(8):
        for gu in range(2):
            exchange(b, gu).wait_send()
    for way in range(2):
        for h in range(2):
            rs_copy(way, 4, 1, h).wait_send()
        for k in (3, 2, 1):
            for q in range(2):
                for h in range(2):
                    rs_copy(way, k, q, h).wait_send()
        for s in (1, 2, 3):
            for h in range(2):
                ag_copy(way, s, h).wait_send()
        ag_copy(way, 4, way).wait_send()


def local(tokens, gate_weight, up_weight, down_weight):
    rows, depth = tokens.shape
    width, columns = down_weight.shape
    anywhere = pl.BlockSpec(memory_space=pl.ANY)
    dma = pltpu.SemaphoreType.DMA
    bf16, f32 = jnp.bfloat16, jnp.float32
    return pl.pallas_call(
        kernel,
        name="gated_block",
        out_shape=jax.ShapeDtypeStruct((rows, columns), f32),
        in_specs=[anywhere] * 4,
        out_specs=pl.BlockSpec(memory_space=pltpu.VMEM),
        scratch_shapes=[
            pltpu.VMEM((2, depth, width), bf16),
            pltpu.VMEM((width, columns), bf16),
            pltpu.VMEM((16, rows, depth), bf16),
            pltpu.VMEM((8, 2, 2, rows, width), f32),
            pltpu.VMEM((8, 2, 2, HALF, width), f32),
            pltpu.VMEM((2, 14, HALF, width), bf16),
            pltpu.VMEM((2, 14, HALF, width), bf16),
            pltpu.VMEM((8, 2, rows, width), bf16),
            pltpu.VMEM((16, rows, columns), bf16),
            pltpu.VMEM((16, rows, columns), bf16),
            dma((4,)), dma((16,)), dma((16,)), dma((16,)), dma((16,)), dma((28,)), dma((28,)),
            dma((14,)), dma((14,)), dma((16,)), dma((16,)), dma((16,)), dma((16,)),
        ],
        compiler_params=pltpu.CompilerParams(
            collective_id=0, has_side_effects=True, vmem_limit_bytes=58 * 1024 * 1024
        ),
        cost_estimate=pl.CostEstimate(
            flops=2 * 16 * rows * depth * 3 * width, bytes_accessed=3 * 2 * depth * width, transcendentals=0
        ),
    )(tokens, gate_weight, up_weight, down_weight)


def solution(mesh):
    placed = (P("gy", "gx"), P("gx", "gy"), P("gx", "gy"), P("gy", "gx"))
    return jax.shard_map(
        local, mesh=mesh, in_specs=placed, out_specs=P("gy", "gx"), check_vma=False
    )
```

time: 301 us -> 101 us (0.34)
  waiting for transfers between devices: 262 us -> 0 us
  Pallas kernels: 0 us -> 98.7 us
  matrix products: 18.6 us -> 0 us
  between operations: 13.2 us -> 0.01 us
  other arithmetic: 7.18 us -> 0 us
    reduce_scatter x2 -> x0, waiting for transfers between devices: 163 us -> none  [the longest x1 83.9 us: local(): lax.psum_scatter(jnp.concatenate([gate_part, up_part], axis=1), 'gx', sca...]
    pallas_call x0 -> x1, Pallas kernels: none -> 98.7 us  [local(): pl.pallas_call(kernel, name='gated_block', out_shape=jax.ShapeDtypeStruct...]
    all_gather x2 -> x0, waiting for transfers between devices: 97.6 us -> none  [the longest x1 55.4 us: local(): all_rows = lax.all_gather(tokens, 'gy', axis=0, tiled=True)]
    dot_general x3 -> x0, matrix products: 18.6 us -> none  [the longest x1 8.9 us: local(): jnp.dot(rows, down_weight, preferred_element_type=jnp.float32)]
    concatenate x1 -> x0, other arithmetic: 5.25 us -> none  [local(): jnp.concatenate([gate_part, up_part], axis=1)]
  transfers between devices with their start and end apart: 4 -> 0, of which waited for: 4 -> 0; matrix products, arithmetic and copies ran while one was open for 0% -> 0% of each run, Pallas kernels for 0% -> 0%
where the time goes in v1:
time: 101 us; the launch traced here: 100 us
  Pallas kernels  98.7 us (98%)
  local copies, waits for them, and re-layouts  1.67 us (2%)
    pallas_call x1, Pallas kernels, local(): pl.pallas_call(kernel, name='gated_block', out_shape=jax.ShapeDtypeStruct...  98.7 us

profile of v1, /device:TPU:1, one launch (start us, length us, event | category | flops | bytes accessed | tf_op | source)
XLA Modules:
  0.0 100.4 jit_solution(13298145894329562246)
XLA Ops:
  0.0 98.7 %gated_block.1 = f32[64,1024]{1,0:T(8,128)} custom-call(bf16[64,1024]{1,0:T(8,128)(2,1)} %tok_hbm.1, bf16[1024,1664]{1,0:T(8,128)(2,1)} %gate_hbm.1, bf16[1024,1664]{1,0:T(8,128)(2,1)} %up_hbm.1, bf16[1664,1024]{1,0:T(8,128)(2,1)} %down_hbm.1), custom_call_target="tpu_custom_call" | custom-call | flops 10468982784 | bytes 10223616 | tf_op jit(solution)/shard_map/gated_block/pallas_call | solution.py:346
  98.7 1.7 %copy.6 = f32[64,1024]{1,0:T(8,128)} copy(f32[64,1024]{1,0:T(8,128)} %gated_block.1) | data formatting | bytes 524288
